TPU v7x, 32 devices: a whole 2x2x4 slice. The times are simulated.
32 devices in a mesh: dp: 4 (over x, core), tensor: 8 (over z, y).
Axes of the slice: x: 2, y: 2, z: 4, core: 2. Of those that a mesh axis runs over, the one named last changes fastest.
Arguments:
- hidden: bfloat16 [1024, 8192], P('dp', 'tensor'), may hold values from -170 to 170, as said below
- neighbour_ids: int32 [16, 2], P('dp'), may hold values from 0 to 127, as said below
- database: bfloat16 [128, 128, 8192], P('dp', None, 'tensor'), may hold values from -6 to 6
- w_query: bfloat16 [8192, 4096], P(None, 'tensor'), may hold values from -0.0625 to 0.0625
- w_key: bfloat16 [8192, 4096], P(None, 'tensor'), may hold values from -0.0625 to 0.0625
- w_value: bfloat16 [8192, 4096], P(None, 'tensor'), may hold values from -0.0625 to 0.0625
- w_out: bfloat16 [4096, 8192], P('tensor'), may hold values from -0.09375 to 0.09375
Outputs:
- mixed: bfloat16 [1024, 8192], P('dp', 'tensor')
Inputs may be any that keep to these rules, and one draw needn't show every extreme that they name: `neighbour_ids`: database block b is held by index b // 32 of dp. Among the 8 neighbour ids of one sequence (the rows of one device), at most 4 belong to the same holder, and in every sequence exactly 4 do. `hidden`: hidden states may be large for some tokens.
All inputs are finite; a program needn't handle non-finite values.
Results may differ from a plain program's by a relative error of at most 0.02.
Values may be sent and summed in bfloat16 or wider, within the bound.
A program may use at most 128 MiB of HBM per device.

v0:
```python
import jax
import jax.numpy as jnp
from jax import lax
from jax.sharding import PartitionSpec as P

HD = 128


def attend(query_rows, key_rows, value_rows, heads_count, group_len):
    tok_count, width = query_rows.shape
    groups = tok_count // group_len
    head_size = width // heads_count
    shifted = jnp.concatenate(
        [query_rows[group_len - 1 :], jnp.zeros((group_len - 1, width), jnp.bfloat16)], 0
    )
    shifted = shifted.reshape(groups, group_len, heads_count, head_size)
    key_block = key_rows.reshape(groups, -1, heads_count, head_size)
    value_block = value_rows.reshape(groups, -1, heads_count, head_size)
    scores = jnp.einsum(
        "cqhd,ckhd->chqk", shifted, key_block, preferred_element_type=jnp.float32
    ) / jnp.sqrt(jnp.float32(head_size))
    top_score = jnp.max(scores, axis=-1, keepdims=True)
    weights_raw = jnp.exp(scores - top_score)
    soft = (weights_raw / jnp.sum(weights_raw, axis=-1, keepdims=True)).astype(jnp.bfloat16)
    blended = jnp.einsum(
        "chqk,ckhd->cqhd", soft, value_block, preferred_element_type=jnp.float32
    ).astype(jnp.bfloat16)
    blended = blended.reshape(tok_count, width)
    return jnp.concatenate(
        [jnp.zeros((group_len - 1, width), jnp.bfloat16), blended[: tok_count - group_len + 1]], 0
    )


def shards(hidden, neighbour_ids, database, w_query, w_key, w_value, w_out):
    dp_count = lax.axis_size("dp")
    tok_rows = hidden.shape[0]
    group_count = neighbour_ids.shape[0]
    per_reader = group_count * neighbour_ids.shape[1]
    capacity = per_reader // 2
    db_count = database.shape[0]
    ret_len = database.shape[1]
    col_count = database.shape[2]
    head_cols = w_query.shape[1]
    heads_local = head_cols // HD
    query_sum = jnp.dot(
        lax.all_gather(hidden, "tensor", axis=1, tiled=True),
        w_query,
        preferred_element_type=jnp.float32,
    )
    query_rows = query_sum.astype(jnp.bfloat16)
    block_ids = neighbour_ids.reshape(per_reader)
    owners = block_ids // db_count
    earlier = jnp.arange(per_reader)[:, None] > jnp.arange(per_reader)[None, :]
    slot_rank = jnp.sum(((owners[:, None] == owners[None, :]) & earlier).astype(jnp.int32), 1)
    slot_range = jnp.arange(capacity, dtype=jnp.int32)
    local_index = block_ids % db_count
    owner_range = jnp.arange(dp_count, dtype=jnp.int32)
    slot_hit = (owners[:, None, None] == owner_range[None, :, None]) & (
        slot_rank[:, None, None] == slot_range[None, None, :]
    )
    request_table = jnp.sum(slot_hit.astype(jnp.int32) * local_index[:, None, None], 0)
    requested = lax.all_to_all(request_table, "dp", split_axis=0, concat_axis=0, tiled=True)
    outgoing = jnp.take(database, requested.reshape(-1), axis=0).reshape(
        dp_count, capacity, ret_len, col_count
    )
    arrived = lax.all_to_all(outgoing, "dp", split_axis=0, concat_axis=0, tiled=True)
    neighbour_rows = jnp.take(
        arrived.reshape(dp_count * capacity, ret_len, col_count),
        owners * capacity + slot_rank,
        axis=0,
    )
    assembled = lax.all_gather(neighbour_rows, "tensor", axis=2, tiled=True).reshape(
        per_reader * ret_len, -1
    )
    key_sum = jnp.dot(assembled, w_key, preferred_element_type=jnp.float32)
    value_sum = jnp.dot(assembled, w_value, preferred_element_type=jnp.float32)
    key_rows = key_sum.astype(jnp.bfloat16)
    value_rows = value_sum.astype(jnp.bfloat16)
    context = attend(query_rows, key_rows, value_rows, heads_local, tok_rows // group_count)
    partial_out = jnp.dot(context, w_out, preferred_element_type=jnp.float32)
    return lax.psum_scatter(
        partial_out.astype(jnp.bfloat16), "tensor", scatter_dimension=1, tiled=True
    )


def solution(mesh):
    placed = (
        P("dp", "tensor"),
        P("dp", None),
        P("dp", None, "tensor"),
        P(None, "tensor"),
        P(None, "tensor"),
        P(None, "tensor"),
        P("tensor", None),
    )
    return jax.shard_map(
        shards, mesh=mesh, in_specs=placed, out_specs=P("dp", "tensor"), check_vma=False
    )
```

profile of v0, /device:TPU:0, one launch (start us, length us, event | category | flops | bytes accessed | tf_op | source)
XLA Modules:
  0.0 448.1 jit_solution(14116617784531274441)
XLA Ops:
  6.5 0.7 all-gather.5.cloned.1.call-update
  7.3 0.8 copy.26
  8.1 0.2 convert_reduce_fusion
  8.5 7.8 %all_to_all.14 = s32[4,1,4]{2,1,0:T(1,128)S(1)} all-to-all(s32[4,1,4]{2,1,0:T(1,128)S(1)} %bitcast.35), channel_id=1, replica_groups=mesh['dp'=4,'tensor'=8] {'dp'}, dimensions={0} | all-to-all | bytes 128 | tf_op jit(solution)/shard_map/all_to_all | solution.py:62
  16.2 0.5 broadcast.320
  16.7 0.7 reduce.3
  17.5 6.5 %gather_fusion = bf16[16,128,1024]{2,1,0:T(8,128)(2,1)} fusion(bf16[32,128,1024]{2,1,0:T(8,128)(2,1)} %param.9, s32[1024]{0:T(1024)S(1)} %pad_clamp_fusion.1), kind=kCustom, calls=%fused_computation | custom fusion | bytes 8388672 | tf_op jit(solution)/shard_map/jit(_take)/gather | solution.py:63
  24.1 4.6 %broadcast_select_fusion = bf16[4,4,128,1024]{3,2,1,0:T(8,128)(2,1)} fusion(bf16[4,4,128,1024]{3,2,1,0:T(8,128)(2,1)} %bitcast.31, pred[4,4]{1,0:T(4,128)(4,1)S(1)} %compare_and_fusion), kind=kLoop, calls=%fused_computation.4 | loop fusion | flops 2097152 | bytes 8388624 | tf_op jit(solution)/shard_map/jit(_take)/select_n | solution.py:63
  28.6 4.9 %all-to-all-start.1 = ((bf16[4,4,128,1024]{3,2,1,0:T(8,128)(2,1)}), bf16[4,4,128,1024]{3,2,1,0:T(8,128)(2,1)}, u32[]{:S(2)}, u32[]{:S(2)}) async-start(bf16[4,4,128,1024]{3,2,1,0:T(8,128)(2,1)} %broadcast_select_fusion), calls=%async_computation.1 | async-start | bytes 8388608 | tf_op jit(solution)/shard_map/all_to_all | solution.py:66
  33.7 48.1 %all-to-all-done.1 = bf16[4,4,128,1024]{3,2,1,0:T(8,128)(2,1)} async-done(((bf16[4,4,128,1024]{3,2,1,0:T(8,128)(2,1)}), bf16[4,4,128,1024]{3,2,1,0:T(8,128)(2,1)}, u32[]{:S(2)}, u32[]{:S(2)}) %all-to-all-start.1) | async-done | bytes 4194336 | tf_op jit(solution)/shard_map/all_to_all | solution.py:66
  81.7 2.9 gather_fusion.1
  84.6 1.6 broadcast_select_fusion.1
  86.3 7.0 %fusion.15 = bf16[256,512]{1,0:T(8,128)(2,1)S(1)} fusion(bf16[256,8192]{1,0:T(8,128)(2,1)} %all-gather.5.cloned.1.call-done, bf16[8192,512]{1,0:T(8,128)(2,1)} %param.10), kind=kOutput, calls=%fused_computation.50 | convolution fusion | flops 2147483648 | bytes 12845056 | tf_op jit(solution)/shard_map/dot_general | solution.py:45
  93.4 220.8 %all-gather.3.cloned.1.call-done = bf16[8,128,8192]{2,1,0:T(8,128)(2,1)} async-done(((bf16[8,128,1024]{2,1,0:T(8,128)(2,1)}), bf16[8,128,8192]{2,1,0:T(8,128)(2,1)}) %all-gather.3.cloned.1.call-update) | async-done | bytes 16777232 | tf_op jit(solution)/shard_map/all_gather | solution.py:72
  314.3 14.8 %convolution_convert_fusion.2 = bf16[1024,512]{1,0:T(8,128)(2,1)S(1)} fusion(bf16[1024,8192]{1,0:T(8,128)(2,1)} %bitcast.36, bf16[8192,512]{1,0:T(8,128)(2,1)} %param.12), kind=kOutput, calls=%fused_computation.7 | convolution fusion | flops 8590458880 | bytes 26214400 | tf_op jit(solution)/shard_map/dot_general | solution.py:76
  329.1 0.3 reshape.305
  329.3 14.8 %convolution_convert_fusion.1 = bf16[1024,512]{1,0:T(8,128)(2,1)S(1)} fusion(bf16[1024,8192]{1,0:T(8,128)(2,1)} %bitcast.37, bf16[8192,512]{1,0:T(8,128)(2,1)} %param.11), kind=kOutput, calls=%fused_computation.6 | convolution fusion | flops 8590458880 | bytes 26214400 | tf_op jit(solution)/shard_map/dot_general | solution.py:75
  344.1 0.3 reshape.307
  344.4 0.5 convolution_multiply_fusion
  344.9 0.4 fusion.14
  345.3 1.9 fusion.3
  347.1 0.2 copy.32
  347.4 7.7 %convolution_convert_fusion = bf16[256,8192]{1,0:T(8,128)(2,1)} fusion(bf16[512,8192]{1,0:T(8,128)(2,1)} %param.13, bf16[193,512]{1,0:T(8,128)(2,1)S(1)} %slice.13), kind=kOutput, calls=%fused_computation.3 | convolution fusion | flops 2149580800 | bytes 12780544 | tf_op jit(solution)/shard_map/dot_general | solution.py:80
  355.1 86.4 %reduce-scatter.2.cloned.1.call-done = bf16[256,1024]{1,0:T(8,128)(2,1)} async-done(((bf16[256,8192]{1,0:T(8,128)(2,1)}), bf16[256,1024]{1,0:T(8,128)(2,1)}) %reduce-scatter.2.cloned.1.call-update) | async-done | bytes 524304 | tf_op jit(solution)/shard_map/reduce_scatter | solution.py:81
  (23 shorter events, 0.8 us)
Async XLA Ops:
  6.5 79.8 %all-gather.5.cloned.1.call-start = ((), (), s32[]{:S(2)}) async-start(), calls=%async_computation.4 | async-start | bytes 4718592 | tf_op jit(solution)/shard_map/all_gather | solution.py:46
  28.6 53.1 %all-to-all-start.1 = ((bf16[4,4,128,1024]{3,2,1,0:T(8,128)(2,1)}), bf16[4,4,128,1024]{3,2,1,0:T(8,128)(2,1)}, u32[]{:S(2)}, u32[]{:S(2)}) async-start(bf16[4,4,128,1024]{3,2,1,0:T(8,128)(2,1)} %broadcast_select_fusion), calls=%async_computation.1 | async-start | bytes 8388608 | tf_op jit(solution)/shard_map/all_to_all | solution.py:66
  33.5 280.8 %all-gather.3.cloned.1.call-start = ((), (), s32[]{:S(2)}) async-start(), calls=%async_computation.3 | async-start | bytes 18874368 | tf_op jit(solution)/shard_map/all_gather | solution.py:72
  86.2 355.3 %reduce-scatter.2.cloned.1.call-start = ((), (), s32[]{:S(2)}) async-start(), calls=%async_computation.5 | async-start | bytes 4718592 | tf_op jit(solution)/shard_map/reduce_scatter | solution.py:81
Sparse Core Ops, SparseCore 0:
  9.5 76.0 all-gather.4
  87.8 226.4 all-gather.2
  355.2 86.2 reduce-scatter.1
where the time goes:
time: 448 us
  waiting for transfers between devices  356 us (79%)
  matrix products  46.5 us (10%)
  between operations  13.2 us (3%)
  local copies, waits for them, and re-layouts  11.9 us (3%)
  blocking collectives  7.76 us (2%)
  other arithmetic  7.61 us (2%)
  starting transfers between devices  4.95 us (1%)
    all_gather x1, waiting for transfers between devices, shards(): lax.all_gather(neighbour_rows, 'tensor', axis=2, tiled=True)  221 us
    reduce_scatter x1, waiting for transfers between devices, shards(): lax.psum_scatter(partial_out.astype(jnp.bfloat16), 'tensor', scatter_dime...  86.4 us
    all_to_all x1, waiting for transfers between devices, shards(): lax.all_to_all(outgoing, 'dp', split_axis=0, concat_axis=0, tiled=True)  48.1 us
    dot_general x1, matrix products, shards(): key_sum = jnp.dot(assembled, w_key, preferred_element_type=jnp.float32)  14.8 us
    dot_general x1, matrix products, shards(): value_sum = jnp.dot(assembled, w_value, preferred_element_type=jnp.float32)  14.8 us
  transfers between devices with their start and end apart: 4, of which 3 were waited for; matrix products, arithmetic and copies ran while one was open for 6% of the time, Pallas kernels for 0%

commit v1 on v0

--- a/solution.py
+++ b/solution.py
@@ -1,7 +1,13 @@
+import functools
+
 import jax
 import jax.numpy as jnp
 from jax import lax
+from jax.experimental import pallas as pl
+from jax.experimental.pallas import tpu as pltpu
 from jax.sharding import PartitionSpec as P
+
+MESH = pl.DeviceIdType.MESH
 
 HD = 128
 
@@ -31,6 +37,334 @@
     )
 
 
+def plane(tensor_count):
+    nz = 4 if tensor_count % 4 == 0 else 1
+    return nz, tensor_count // nz
+
+
+def gather_project(
+    nz, ny, x_ref, wk_ref, wv_ref, k_ref, v_ref,
+    held, wk_held, wv_held, total, send_sem, recv_sem, local_sem,
+):
+    chunks, rows, feats = x_ref.shape
+    cols = wk_ref.shape[1]
+    me = lax.axis_index("tensor")
+    z, y = me // ny, me % ny
+    up, down, right, left = z + 1 < nz, z >= 1, y + 1 < ny, y >= 1
+
+    own_copy = pltpu.make_async_copy(x_ref, held.at[me], local_sem.at[0])
+    own_copy.start()
+    wk_copy = pltpu.make_async_copy(wk_ref, wk_held, local_sem.at[1])
+    wk_copy.start()
+    wv_copy = pltpu.make_async_copy(wv_ref, wv_held, local_sem.at[2])
+    wv_copy.start()
+
+    barrier = pltpu.get_barrier_semaphore()
+    sides = ((up, ny), (down, -ny), (right, 1), (left, -1))
+    for there, step in sides:
+        @pl.when(there)
+        def _():
+            pl.semaphore_signal(
+                barrier, inc=1, device_id={"tensor": me + step}, device_id_type=MESH
+            )
+    pl.semaphore_wait(barrier, sum(there.astype(jnp.int32) for there, _ in sides))
+
+    def move(side, shard, c):
+        return pltpu.make_async_remote_copy(
+            src_ref=held.at[shard, c],
+            dst_ref=held.at[shard, c],
+            send_sem=send_sem.at[side, shard, c],
+            recv_sem=recv_sem.at[shard, c],
+            device_id={"tensor": me + sides[side][1]},
+            device_id_type=MESH,
+        )
+
+    def send(side, shard, c, cond):
+        @pl.when(cond & sides[side][0])
+        def _():
+            move(side, shard, c).start()
+
+    def landed(shard, c):
+        move(0, shard, c).wait_recv()
+
+    total[...] = jnp.zeros_like(total)
+    own_copy.wait()
+
+    def column(e):
+        step = (e + 1) // 2
+        above = e % 2 == 0
+        zc = jnp.where(above, z + step, z - step)
+        return zc, above, step, (zc >= 0) & (zc < nz) & (e >= 0) & (e < 2 * nz - 1)
+
+    def project(shard):
+        w_rows = pl.ds(pl.multiple_of(shard * feats, feats), feats)
+
+        @pl.loop(0, chunks)
+        def _(c):
+            block = held[shard, c]
+            total[c, :, :cols] += jnp.dot(
+                block, wk_held[w_rows, :], preferred_element_type=jnp.float32
+            )
+            total[c, :, cols:] += jnp.dot(
+                block, wv_held[w_rows, :], preferred_element_type=jnp.float32
+            )
+
+    def event(e, carry):
+        zc, above, step, valid = column(e)
+
+        @pl.when(valid)
+        def _():
+            shard = zc * ny + y
+            for c in range(chunks):
+                @pl.when(step > 0)
+                def _():
+                    landed(shard, c)
+
+                send(0, shard, c, (step == 0) | jnp.logical_not(above))
+                send(1, shard, c, above)
+                send(2, shard, c, True)
+                send(3, shard, c, True)
+
+            @pl.when(step == 0)
+            def _():
+                wk_copy.wait()
+                wv_copy.wait()
+
+            project(shard)
+
+        zl, _, _, late = column(e - 2)
+        for m in range(1, ny):
+            for sign in (-1, 1):
+                yc = y + sign * m
+
+                @pl.when(late & (yc >= 0) & (yc < ny))
+                def _():
+                    shard = zl * ny + yc
+                    for c in range(chunks):
+                        landed(shard, c)
+                        if ny > 2:
+                            send(2 if sign < 0 else 3, shard, c, True)
+                    project(shard)
+        return carry
+
+    lax.fori_loop(0, 2 * nz + 1, event, 0)
+
+    k_ref[...] = total[:, :, :cols].astype(jnp.bfloat16)
+    v_ref[...] = total[:, :, cols:].astype(jnp.bfloat16)
+
+    def finish(shard, carry):
+        zs, ys = shard // ny, shard % ny
+        mine = ys == y
+        went = (mine & (zs <= z), mine & (zs >= z), ys <= y, ys >= y)
+        for side in range(4):
+            @pl.when(went[side] & sides[side][0])
+            def _():
+                for c in range(chunks):
+                    move(side, shard, c).wait_send()
+        return carry
+
+    lax.fori_loop(0, nz * ny, finish, 0)
+
+
+def neighbour_keys(rows, w_key, w_value, chunks):
+    tensor_count = lax.axis_size("tensor")
+    nz, ny = plane(tensor_count)
+    row_count, feats = rows.shape
+    cols = w_key.shape[1]
+    per = row_count // chunks
+    out = jax.ShapeDtypeStruct((chunks, per, cols), jnp.bfloat16)
+    keys, values = pl.pallas_call(
+        functools.partial(gather_project, nz, ny),
+        out_shape=(out, out),
+        in_specs=[pl.BlockSpec(memory_space=pl.ANY)] * 3,
+        out_specs=(pl.BlockSpec(memory_space=pltpu.VMEM),) * 2,
+        scratch_shapes=[
+            pltpu.VMEM((tensor_count, chunks, per, feats), jnp.bfloat16),
+            pltpu.VMEM(w_key.shape, jnp.bfloat16),
+            pltpu.VMEM(w_value.shape, jnp.bfloat16),
+            pltpu.VMEM((chunks, per, 2 * cols), jnp.float32),
+            pltpu.SemaphoreType.DMA((4, tensor_count, chunks)),
+            pltpu.SemaphoreType.DMA((tensor_count, chunks)),
+            pltpu.SemaphoreType.DMA((3,)),
+        ],
+        compiler_params=pltpu.CompilerParams(
+            collective_id=0, has_side_effects=True, vmem_limit_bytes=56 * 2**20
+        ),
+        cost_estimate=pl.CostEstimate(
+            flops=4 * row_count * feats * tensor_count * cols,
+            bytes_accessed=4 * w_key.size,
+            transcendentals=0,
+        ),
+    )(rows.reshape(chunks, per, feats), w_key, w_value)
+    return keys.reshape(row_count, cols), values.reshape(row_count, cols)
+
+
+def project_scatter(
+    nz, ny, ctx_ref, w_ref, out_ref, w_held, outgoing, from_y, from_z,
+    total, send_sem, recv_y, recv_z, local_sem,
+):
+    feats = out_ref.shape[1]
+    count = nz * ny
+    me = lax.axis_index("tensor")
+    z, y = me // ny, me % ny
+    up, down, right, left = z + 1 < nz, z >= 1, y + 1 < ny, y >= 1
+    sides = ((up, ny), (down, -ny), (right, 1), (left, -1))
+
+    def load(dest):
+        columns = pl.ds(pl.multiple_of(dest * feats, feats), feats)
+        return pltpu.make_async_copy(
+            w_ref.at[:, columns], w_held.at[dest], local_sem.at[dest]
+        )
+
+    def column(e):
+        step = (e + 1) // 2
+        above = e % 2 == 0
+        zc = jnp.where(above, z + step, z - step)
+        return zc, above, (zc >= 0) & (zc < nz) & (e >= 0) & (e < 2 * nz - 1)
+
+    def fetch(i, carry):
+        zc, _, valid = column(2 * nz - 2 - i)
+
+        @pl.when(valid)
+        def _():
+            for off in range(1, ny + 1):
+                load(zc * ny + (y + off) % ny).start()
+        return carry
+
+    lax.fori_loop(0, 2 * nz - 1, fetch, 0)
+
+    barrier = pltpu.get_barrier_semaphore()
+    for there, step in sides:
+        @pl.when(there)
+        def _():
+            pl.semaphore_signal(
+                barrier, inc=1, device_id={"tensor": me + step}, device_id_type=MESH
+            )
+    pl.semaphore_wait(barrier, sum(there.astype(jnp.int32) for there, _ in sides))
+
+    def along_y(side, dest):
+        return pltpu.make_async_remote_copy(
+            src_ref=outgoing.at[dest],
+            dst_ref=from_y.at[side, dest],
+            send_sem=send_sem.at[dest],
+            recv_sem=recv_y.at[side, dest],
+            device_id={"tensor": me + (1 if side == 0 else -1)},
+            device_id_type=MESH,
+        )
+
+    def along_z(side, dest):
+        return pltpu.make_async_remote_copy(
+            src_ref=outgoing.at[dest],
+            dst_ref=from_z.at[side, dest // ny],
+            send_sem=send_sem.at[dest],
+            recv_sem=recv_z.at[side, dest // ny],
+            device_id={"tensor": me + (ny if side == 0 else -ny)},
+            device_id_type=MESH,
+        )
+
+    def own_share(dest):
+        load(dest).wait()
+        return jnp.dot(ctx_ref[...], w_held[dest], preferred_element_type=jnp.float32)
+
+    def event(i, carry):
+        zc, _, valid = column(2 * nz - 2 - i)
+        for m in range(ny - 1, 0, -1):
+            for side in (0, 1):
+                yc = y + m if side == 0 else y - m
+
+                @pl.when(valid & (yc >= 0) & (yc < ny))
+                def _():
+                    dest = zc * ny + yc
+                    share = own_share(dest)
+                    outgoing[dest] = share.astype(jnp.bfloat16)
+                    if ny > 2:
+                        @pl.when(left if side == 0 else right)
+                        def _():
+                            along_y(side, dest).wait_recv()
+                            outgoing[dest] = (
+                                share + from_y[side, dest].astype(jnp.float32)
+                            ).astype(jnp.bfloat16)
+                    along_y(side, dest).start()
+
+        zl, above, late = column(2 * nz - 2 - i + 2)
+
+        @pl.when(late)
+        def _():
+            dest = zl * ny + y
+            share = own_share(dest)
+            total[...] = share
+            for side, there in ((0, left), (1, right)):
+                @pl.when(there)
+                def _():
+                    along_y(side, dest).wait_recv()
+                    total[...] += from_y[side, dest].astype(jnp.float32)
+            for side, there in ((0, down & (zl >= z)), (1, up & (zl <= z))):
+                @pl.when(there)
+                def _():
+                    along_z(side, dest).wait_recv()
+                    total[...] += from_z[side, zl].astype(jnp.float32)
+
+            @pl.when(zl == z)
+            def _():
+                out_ref[...] = total[...].astype(jnp.bfloat16)
+
+            @pl.when(zl != z)
+            def _():
+                outgoing[dest] = total[...].astype(jnp.bfloat16)
+
+            @pl.when(zl > z)
+            def _():
+                along_z(0, dest).start()
+
+            @pl.when(zl < z)
+            def _():
+                along_z(1, dest).start()
+        return carry
+
+    lax.fori_loop(0, 2 * nz + 1, event, 0)
+
+    def finish(dest, carry):
+        @pl.when(dest != me)
+        def _():
+            along_y(0, dest).wait_send()
+        return carry
+
+    lax.fori_loop(0, count, finish, 0)
+
+
+def project_out(context, w_out):
+    tensor_count = lax.axis_size("tensor")
+    nz, ny = plane(tensor_count)
+    rows, depth = context.shape
+    feats = w_out.shape[1] // tensor_count
+    return pl.pallas_call(
+        functools.partial(project_scatter, nz, ny),
+        out_shape=jax.ShapeDtypeStruct((rows, feats), jnp.bfloat16),
+        in_specs=[
+            pl.BlockSpec(memory_space=pltpu.VMEM),
+            pl.BlockSpec(memory_space=pl.ANY),
+        ],
+        out_specs=pl.BlockSpec(memory_space=pltpu.VMEM),
+        scratch_shapes=[
+            pltpu.VMEM((tensor_count, depth, feats), jnp.bfloat16),
+            pltpu.VMEM((tensor_count, rows, feats), jnp.bfloat16),
+            pltpu.VMEM((2, tensor_count, rows, feats), jnp.bfloat16),
+            pltpu.VMEM((2, nz, rows, feats), jnp.bfloat16),
+            pltpu.VMEM((rows, feats), jnp.float32),
+            pltpu.SemaphoreType.DMA((tensor_count,)),
+            pltpu.SemaphoreType.DMA((2, tensor_count)),
+            pltpu.SemaphoreType.DMA((2, nz)),
+            pltpu.SemaphoreType.DMA((tensor_count,)),
+        ],
+        compiler_params=pltpu.CompilerParams(
+            collective_id=1, has_side_effects=True, vmem_limit_bytes=48 * 2**20
+        ),
+        cost_estimate=pl.CostEstimate(
+            flops=2 * rows * w_out.size, bytes_accessed=2 * w_out.size, transcendentals=0
+        ),
+    )(context, w_out)
+
+
 def shards(hidden, neighbour_ids, database, w_query, w_key, w_value, w_out):
     dp_count = lax.axis_size("dp")
     tok_rows = hidden.shape[0]
@@ -69,18 +403,13 @@
         owners * capacity + slot_rank,
         axis=0,
     )
-    assembled = lax.all_gather(neighbour_rows, "tensor", axis=2, tiled=True).reshape(
-        per_reader * ret_len, -1
-    )
-    key_sum = jnp.dot(assembled, w_key, preferred_element_type=jnp.float32)
-    value_sum = jnp.dot(assembled, w_value, preferred_element_type=jnp.float32)
-    key_rows = key_sum.astype(jnp.bfloat16)
-    value_rows = value_sum.astype(jnp.bfloat16)
+    key_rows, value_rows = neighbour_keys(
+        neighbour_rows.reshape(per_reader * ret_len, col_count), w_key, w_value, group_count
+    )
     context = attend(query_rows, key_rows, value_rows, heads_local, tok_rows // group_count)
-    partial_out = jnp.dot(context, w_out, preferred_element_type=jnp.float32)
-    return lax.psum_scatter(
-        partial_out.astype(jnp.bfloat16), "tensor", scatter_dimension=1, tiled=True
-    )
+    skipped = (tok_rows // group_count - 1) // 16 * 16
+    mixed = project_out(context[skipped:], w_out)
+    return jnp.concatenate([jnp.zeros((skipped, mixed.shape[1]), mixed.dtype), mixed], 0)
 
 
 def solution(mesh):

time: 448 us -> 337 us (0.75)
  waiting for transfers between devices: 356 us -> 48.6 us
  Pallas kernels: 0 us -> 232 us
  matrix products: 46.5 us -> 9.38 us
    pallas_call x0 -> x2, Pallas kernels: none -> 232 us  [the longest x1 189 us: neighbour_keys(): pl.pallas_call(functools.partial(gather_project, nz, ny), out_shape=(out,...]
    all_gather x1 -> x0, waiting for transfers between devices: 221 us -> none  [shards(): lax.all_gather(neighbour_rows, 'tensor', axis=2, tiled=True)]
    reduce_scatter x1 -> x0, waiting for transfers between devices: 86.4 us -> none  [shards(): lax.psum_scatter(partial_out.astype(jnp.bfloat16), 'tensor', scatter_dime...]
    dot_general x3 -> x0, matrix products: 37.2 us -> none  [the longest x1 14.8 us: shards(): key_sum = jnp.dot(assembled, w_key, preferred_element_type=jnp.float32)]
  transfers between devices with their start and end apart: 4 -> 2, of which waited for: 3 -> 1; matrix products, arithmetic and copies ran while one was open for 6% -> 6% of each run, Pallas kernels for 0% -> 56%
where the time goes in v1:
time: 337 us; the launch traced here: 336 us
  Pallas kernels  232 us (69%)
  waiting for transfers between devices  48.6 us (14%)
  between operations  13.5 us (4%)
  local copies, waits for them, and re-layouts  12.7 us (4%)
  matrix products  9.38 us (3%)
  blocking collectives  7.76 us (2%)
  other arithmetic  7.67 us (2%)
  starting transfers between devices  4.96 us (1%)
    pallas_call x1, Pallas kernels, neighbour_keys(): pl.pallas_call(functools.partial(gather_project, nz, ny), out_shape=(out,...  189 us
    all_to_all x1, waiting for transfers between devices, shards(): lax.all_to_all(outgoing, 'dp', split_axis=0, concat_axis=0, tiled=True)  47.8 us
    pallas_call x1, Pallas kernels, project_out(): pl.pallas_call(functools.partial(project_scatter, nz, ny), out_shape=jax....  42.1 us
    all_to_all x1, blocking collectives, shards(): lax.all_to_all(request_table, 'dp', split_axis=0, concat_axis=0, tiled=True)  7.76 us
    dot_general x1, matrix products, shards(): jnp.dot(lax.all_gather(hidden, 'tensor', axis=1, tiled=True), w_query, pr...  7.04 us
  transfers between devices with their start and end apart: 2, of which 1 were waited for; matrix products, arithmetic and copies ran while one was open for 6% of the time, Pallas kernels for 56%

profile of v1, /device:TPU:0, one launch (start us, length us, event | category | flops | bytes accessed | tf_op | source)
XLA Modules:
  0.0 336.1 jit_solution(15683618266408660106)
XLA Ops:
  6.5 0.7 all-gather.2.cloned.1.call-update
  7.3 0.8 copy.41
  8.1 0.2 convert_reduce_fusion
  8.3 0.2 select_reduce_fusion
  8.5 7.8 %all_to_all.14 = s32[4,1,4]{2,1,0:T(1,128)S(1)} all-to-all(s32[4,1,4]{2,1,0:T(1,128)S(1)} %bitcast.49), channel_id=1, replica_groups=mesh['dp'=4,'tensor'=8] {'dp'}, dimensions={0} | all-to-all | bytes 128 | tf_op jit(solution)/shard_map/all_to_all | solution.py:396
  16.2 0.5 broadcast.340
  16.7 0.7 reduce.3
  17.4 0.1 reshape.297
  17.5 6.5 %gather_fusion = bf16[16,128,1024]{2,1,0:T(8,128)(2,1)} fusion(bf16[32,128,1024]{2,1,0:T(8,128)(2,1)} %param.9, s32[1024]{0:T(1024)S(1)} %pad_clamp_fusion.1), kind=kCustom, calls=%fused_computation | custom fusion | bytes 8388672 | tf_op jit(solution)/shard_map/jit(_take)/gather | solution.py:397
  24.1 4.6 %broadcast_select_fusion = bf16[4,4,128,1024]{3,2,1,0:T(8,128)(2,1)} fusion(bf16[4,4,128,1024]{3,2,1,0:T(8,128)(2,1)} %bitcast.44, pred[4,4]{1,0:T(4,128)(4,1)S(1)} %compare_and_fusion), kind=kLoop, calls=%fused_computation.3 | loop fusion | flops 2097152 | bytes 8388624 | tf_op jit(solution)/shard_map/jit(_take)/select_n | solution.py:397
  28.7 5.0 %all-to-all-start.1 = ((bf16[4,4,128,1024]{3,2,1,0:T(8,128)(2,1)}), bf16[4,4,128,1024]{3,2,1,0:T(8,128)(2,1)}, u32[]{:S(2)}, u32[]{:S(2)}) async-start(bf16[4,4,128,1024]{3,2,1,0:T(8,128)(2,1)} %broadcast_select_fusion), calls=%async_computation.1 | async-start | bytes 8388608 | tf_op jit(solution)/shard_map/all_to_all | solution.py:400
  33.8 0.1 copy.46
  34.1 47.8 %all-to-all-done.1 = bf16[4,4,128,1024]{3,2,1,0:T(8,128)(2,1)} async-done(((bf16[4,4,128,1024]{3,2,1,0:T(8,128)(2,1)}), bf16[4,4,128,1024]{3,2,1,0:T(8,128)(2,1)}, u32[]{:S(2)}, u32[]{:S(2)}) %all-to-all-start.1) | async-done | bytes 4194336 | tf_op jit(solution)/shard_map/all_to_all | solution.py:400
  81.9 2.9 gather_fusion.1
  84.8 1.6 bitcast_select_fusion.x_ref
  86.4 189.4 %shard_map.73 = (bf16[4,256,512]{2,1,0:T(8,128)(2,1)}, bf16[4,256,512]{2,1,0:T(8,128)(2,1)}) custom-call(bf16[4,256,1024]{2,1,0:T(8,128)(2,1)} %bitcast_select_fusion.x_ref, bf16[8192,512]{1,0:T(8,128)(2,1)} %wk_ref.1, bf16[8192,512]{1,0:T(8,128)(2,1)} %wv_ref.1), custom_call_target="tpu_custom_call" | custom-call | flops 17179869184 | bytes 16777216 | tf_op jit(solution)/shard_map/pallas_call | solution.py:176
  275.8 7.0 %fusion.19 = bf16[256,512]{1,0:T(8,128)(2,1)S(1)} fusion(bf16[256,8192]{1,0:T(8,128)(2,1)} %all-gather.2.cloned.1.call-done, bf16[8192,512]{1,0:T(8,128)(2,1)} %param.10), kind=kOutput, calls=%fused_computation.58 | convolution fusion | flops 2147483648 | bytes 12845056 | tf_op jit(solution)/shard_map/dot_general | solution.py:379
  283.1 0.5 convolution_multiply_fusion
  283.6 0.4 fusion.18
  283.9 0.2 copy-done.1
  284.1 1.9 fusion.3
  286.0 0.2 copy.52
  286.3 42.1 %shard_map.74 = bf16[208,1024]{1,0:T(8,128)(2,1)S(1)} custom-call(bf16[208,512]{1,0:T(8,128)(2,1)S(1)} %pad_slice_fusion.ctx_ref, bf16[512,8192]{1,0:T(8,128)(2,1)} %w_ref.1), custom_call_target="tpu_custom_call" | custom-call | flops 1744830464 | bytes 8388608 | tf_op jit(solution)/shard_map/pallas_call | solution.py:340
  328.4 0.9 concatenate.11
  (23 shorter events, 0.7 us)
Async XLA Ops:
  6.5 269.3 %all-gather.2.cloned.1.call-start = ((), (), s32[]{:S(2)}) async-start(), calls=%async_computation.2 | async-start | bytes 4718592 | tf_op jit(solution)/shard_map/all_gather | solution.py:380
  28.7 53.2 %all-to-all-start.1 = ((bf16[4,4,128,1024]{3,2,1,0:T(8,128)(2,1)}), bf16[4,4,128,1024]{3,2,1,0:T(8,128)(2,1)}, u32[]{:S(2)}, u32[]{:S(2)}) async-start(bf16[4,4,128,1024]{3,2,1,0:T(8,128)(2,1)} %broadcast_select_fusion), calls=%async_computation.1 | async-start | bytes 8388608 | tf_op jit(solution)/shard_map/all_to_all | solution.py:400
  275.8 7.3 %copy-start = (bf16[4,256,512]{2,1,0:T(8,128)(2,1)S(1)}, bf16[4,256,512]{2,1,0:T(8,128)(2,1)}, u32[]{:S(2)}) copy-start(bf16[4,256,512]{2,1,0:T(8,128)(2,1)} %get-tuple-element.8) | copy-start | bytes 3145732
  282.9 1.2 copy-start.1
Sparse Core Ops, SparseCore 0:
  9.5 76.0 all-gather.1

commit v2 on v1

--- a/solution.py
+++ b/solution.py
@@ -13,28 +13,26 @@
 
 
 def attend(query_rows, key_rows, value_rows, heads_count, group_len):
-    tok_count, width = query_rows.shape
-    groups = tok_count // group_len
+    width = query_rows.shape[1]
+    groups = query_rows.shape[0] // group_len
     head_size = width // heads_count
-    shifted = jnp.concatenate(
-        [query_rows[group_len - 1 :], jnp.zeros((group_len - 1, width), jnp.bfloat16)], 0
-    )
-    shifted = shifted.reshape(groups, group_len, heads_count, head_size)
+    shifted = query_rows.reshape(groups, group_len, heads_count, head_size)
     key_block = key_rows.reshape(groups, -1, heads_count, head_size)
     value_block = value_rows.reshape(groups, -1, heads_count, head_size)
     scores = jnp.einsum(
         "cqhd,ckhd->chqk", shifted, key_block, preferred_element_type=jnp.float32
     ) / jnp.sqrt(jnp.float32(head_size))
-    top_score = jnp.max(scores, axis=-1, keepdims=True)
-    weights_raw = jnp.exp(scores - top_score)
-    soft = (weights_raw / jnp.sum(weights_raw, axis=-1, keepdims=True)).astype(jnp.bfloat16)
+    soft = softmax(scores)
     blended = jnp.einsum(
         "chqk,ckhd->cqhd", soft, value_block, preferred_element_type=jnp.float32
     ).astype(jnp.bfloat16)
-    blended = blended.reshape(tok_count, width)
-    return jnp.concatenate(
-        [jnp.zeros((group_len - 1, width), jnp.bfloat16), blended[: tok_count - group_len + 1]], 0
-    )
+    return blended.reshape(groups * group_len, width)
+
+
+def softmax(scores):
+    top_score = jnp.max(scores, axis=-1, keepdims=True)
+    weights_raw = jnp.exp(scores - top_score)
+    return (weights_raw / jnp.sum(weights_raw, axis=-1, keepdims=True)).astype(jnp.bfloat16)
 
 
 def plane(tensor_count):
@@ -376,12 +374,20 @@
     col_count = database.shape[2]
     head_cols = w_query.shape[1]
     heads_local = head_cols // HD
-    query_sum = jnp.dot(
-        lax.all_gather(hidden, "tensor", axis=1, tiled=True),
-        w_query,
-        preferred_element_type=jnp.float32,
-    )
-    query_rows = query_sum.astype(jnp.bfloat16)
+    group_len = tok_rows // group_count
+    skipped = (group_len - 1) // 16 * 16
+    own_head = (
+        jnp.arange(head_cols)[None, :] // HD == jnp.arange(heads_local)[:, None]
+    )
+    last_hidden = lax.all_gather(hidden[tok_rows - 16 :], "tensor", axis=1, tiled=True)
+    last_query = jnp.dot(last_hidden, w_query, preferred_element_type=jnp.float32)
+    last_query = jnp.where(own_head, last_query[15:].astype(jnp.bfloat16), 0)
+    lifted = lax.dot_general(
+        last_query, w_key, (((1,), (1,)), ((), ())), preferred_element_type=jnp.float32
+    ).astype(jnp.bfloat16)
+    lifted = lax.all_gather(lifted, "tensor", axis=0, tiled=True)
+    late_hidden, lifted = lax.optimization_barrier((hidden[skipped:], lifted))
+    all_hidden = lax.all_gather(late_hidden, "tensor", axis=1, tiled=True)
     block_ids = neighbour_ids.reshape(per_reader)
     owners = block_ids // db_count
     earlier = jnp.arange(per_reader)[:, None] > jnp.arange(per_reader)[None, :]
@@ -394,7 +400,7 @@
     )
     request_table = jnp.sum(slot_hit.astype(jnp.int32) * local_index[:, None, None], 0)
     requested = lax.all_to_all(request_table, "dp", split_axis=0, concat_axis=0, tiled=True)
-    outgoing = jnp.take(database, requested.reshape(-1), axis=0).reshape(
+    outgoing = jnp.take(database, requested.reshape(-1), axis=0, mode="clip").reshape(
         dp_count, capacity, ret_len, col_count
     )
     arrived = lax.all_to_all(outgoing, "dp", split_axis=0, concat_axis=0, tiled=True)
@@ -402,13 +408,43 @@
         arrived.reshape(dp_count * capacity, ret_len, col_count),
         owners * capacity + slot_rank,
         axis=0,
-    )
-    key_rows, value_rows = neighbour_keys(
-        neighbour_rows.reshape(per_reader * ret_len, col_count), w_key, w_value, group_count
-    )
-    context = attend(query_rows, key_rows, value_rows, heads_local, tok_rows // group_count)
-    skipped = (tok_rows // group_count - 1) // 16 * 16
-    mixed = project_out(context[skipped:], w_out)
+        mode="clip",
+    )
+    neighbour_rows = neighbour_rows.reshape(per_reader * ret_len, col_count)
+    full_rows = (group_count - 1) * (per_reader // group_count) * ret_len
+    last_rows = neighbour_rows[full_rows:]
+    place = lax.axis_index("tensor")
+    lifted = lax.dynamic_slice_in_dim(lifted, place * col_count, col_count, 1)
+    last_part = lax.dot_general(
+        lifted, last_rows, (((1,), (1,)), ((), ())), preferred_element_type=jnp.float32
+    )
+    first_rows, last_part = lax.optimization_barrier((neighbour_rows[:full_rows], last_part))
+    last_scores = lax.psum(last_part, "tensor")
+    key_rows, value_rows = neighbour_keys(first_rows, w_key, w_value, group_count - 1)
+    key_rows, last_scores = lax.optimization_barrier((key_rows, last_scores))
+    last_soft = softmax(last_scores / jnp.sqrt(jnp.float32(HD)))
+    last_mix = jnp.dot(
+        last_soft, last_rows, preferred_element_type=jnp.float32
+    ).astype(jnp.bfloat16)
+    last_mix = lax.all_gather(last_mix, "tensor", axis=1, tiled=True)
+    key_rows, all_hidden = lax.optimization_barrier((key_rows, all_hidden))
+    query_rows = jnp.dot(
+        all_hidden, w_query, preferred_element_type=jnp.float32
+    ).astype(jnp.bfloat16)
+    lead = group_len - 1 - skipped
+    blended = attend(query_rows[lead:-1], key_rows, value_rows, heads_local, group_len)
+    last_mix = lax.dynamic_slice_in_dim(last_mix, place * heads_local, heads_local, 0)
+    last_context = jnp.dot(last_mix, w_value, preferred_element_type=jnp.float32)
+    last_context = jnp.sum(jnp.where(own_head, last_context, 0), 0, keepdims=True)
+    context = jnp.concatenate(
+        [
+            jnp.zeros((lead, head_cols), jnp.bfloat16),
+            blended,
+            last_context.astype(jnp.bfloat16),
+        ],
+        0,
+    )
+    mixed = project_out(context, w_out)
     return jnp.concatenate([jnp.zeros((skipped, mixed.shape[1]), mixed.dtype), mixed], 0)
 
 

time: 337 us -> 417 us (1.24)
  blocking collectives: 7.76 us -> 139 us
  Pallas kernels: 232 us -> 170 us
  matrix products: 9.38 us -> 23.5 us
  other arithmetic: 7.67 us -> 1.8 us
    all_gather x0 -> x3, blocking collectives: none -> 95.1 us  [the longest x1 32.5 us: shards(): lax.all_gather(hidden[tok_rows - 16:], 'tensor', axis=1, tiled=True)]
    pallas_call x1, Pallas kernels: 189 us -> 135 us  [neighbour_keys(): pl.pallas_call(functools.partial(gather_project, nz, ny), out_shape=(out,...]
    psum x0 -> x1, blocking collectives: none -> 37.5 us  [shards(): last_scores = lax.psum(last_part, 'tensor')]
    dot_general x1 -> x6, matrix products: 7.04 us -> 21.7 us  [the longest x1 6.4 us: shards(): jnp.dot(all_hidden, w_query, preferred_element_type=jnp.float32)]
    pallas_call x1, Pallas kernels: 42.1 us -> 35.3 us  [project_out(): pl.pallas_call(functools.partial(project_scatter, nz, ny), out_shape=jax....]
    select_n x4 -> x1, other arithmetic: 6.25 us -> 0.01 us  [shards(): jnp.arange(head_cols)[None, :] // HD == jnp.arange(heads_local)[:, None]]
  transfers between devices with their start and end apart: 2 -> 2, of which waited for: 1 -> 1; matrix products, arithmetic and copies ran while one was open for 6% -> 4% of each run, Pallas kernels for 56% -> 32%
where the time goes in v2:
time: 417 us
  Pallas kernels  170 us (41%)
  blocking collectives  139 us (33%)
  waiting for transfers between devices  48.1 us (12%)
  matrix products  23.5 us (6%)
  local copies, waits for them, and re-layouts  15.6 us (4%)
  between operations  13.6 us (3%)
  starting transfers between devices  4.86 us (1%)
    pallas_call x1, Pallas kernels, neighbour_keys(): pl.pallas_call(functools.partial(gather_project, nz, ny), out_shape=(out,...  135 us
    all_to_all x1, waiting for transfers between devices, shards(): lax.all_to_all(outgoing, 'dp', split_axis=0, concat_axis=0, tiled=True)  48.1 us
    psum x1, blocking collectives, shards(): last_scores = lax.psum(last_part, 'tensor')  37.5 us
    pallas_call x1, Pallas kernels, project_out(): pl.pallas_call(functools.partial(project_scatter, nz, ny), out_shape=jax....  35.3 us
    all_gather x1, blocking collectives, shards(): lax.all_gather(hidden[tok_rows - 16:], 'tensor', axis=1, tiled=True)  32.5 us
    all_gather x1, blocking collectives, shards(): last_mix = lax.all_gather(last_mix, 'tensor', axis=1, tiled=True)  31.4 us
    all_gather x1, blocking collectives, shards(): lifted = lax.all_gather(lifted, 'tensor', axis=0, tiled=True)  31.2 us
  transfers between devices with their start and end apart: 2, of which 1 were waited for; matrix products, arithmetic and copies ran while one was open for 4% of the time, Pallas kernels for 32%

profile of v2, /device:TPU:0, one launch (start us, length us, event | category | flops | bytes accessed | tf_op | source)
XLA Modules:
  0.0 416.8 jit_solution(11113475214498187868)
XLA Ops:
  6.5 0.8 slice.28
  7.3 1.8 slice.27
  9.1 32.5 %all_gather.12 = bf16[16,8192]{1,0:T(8,128)(2,1)S(1)} all-gather(bf16[16,1024]{1,0:T(8,128)(2,1)S(1)} %slice.28), channel_id=1, replica_groups=mesh['dp'=4,'tensor'=8] {'tensor'}, dimensions={1}, use_global_device_ids=true | all-gather | bytes 294912 | tf_op jit(solution)/shard_map/all_gather | solution.py:382
  41.6 4.6 %fusion.35 = bf16[16,512]{1,0:T(8,128)(2,1)S(1)} fusion(bf16[16,8192]{1,0:T(8,128)(2,1)S(1)} %all_gather.12, bf16[8192,512]{1,0:T(8,128)(2,1)} %param.10), kind=kOutput, calls=%fused_computation.71 | convolution fusion | flops 134217728 | bytes 8667136 | tf_op jit(solution)/shard_map/dot_general | solution.py:383
  46.2 5.6 %fusion.1 = bf16[1,4,8192]{2,1,0:T(4,128)(2,1)S(1)} fusion(bf16[8192,512]{1,0:T(8,128)(2,1)} %wk_ref.1, s32[512]{0:T(512)S(1)} %add_select_fusion, bf16[512]{0:T(512)(128)(2,1)S(1)} %fusion.24), kind=kOutput, calls=%fused_computation.4 | convolution fusion | flops 33591296 | bytes 8457216 | tf_op jit(solution)/shard_map/dot_general | solution.py:385
  51.9 31.2 %all-gather = bf16[8,4,8192]{2,1,0:T(4,128)(2,1)S(1)} all-gather(bf16[1,4,8192]{2,1,0:T(4,128)(2,1)S(1)} %fusion.1), channel_id=1, replica_groups=mesh['dp'=4,'tensor'=8] {'tensor'}, dimensions={0}, use_global_device_ids=true | all-gather | bytes 589824 | tf_op jit(solution)/shard_map/all_gather | solution.py:388
  83.7 6.3 %all_to_all.14 = s32[4,1,4]{2,1,0:T(1,128)S(1)} all-to-all(s32[4,1,4]{2,1,0:T(1,128)S(1)} %bitcast.48), channel_id=1, replica_groups=mesh['dp'=4,'tensor'=8] {'dp'}, dimensions={0} | all-to-all | bytes 128 | tf_op jit(solution)/shard_map/all_to_all | solution.py:402
  90.1 0.6 broadcast.268
  90.6 0.7 reduce.5
  91.5 6.4 %gather_fusion = bf16[16,128,1024]{2,1,0:T(8,128)(2,1)} fusion(bf16[32,128,1024]{2,1,0:T(8,128)(2,1)} %param.9, s32[1024]{0:T(1024)S(1)} %pad_clamp_fusion.1), kind=kCustom, calls=%fused_computation | custom fusion | bytes 8388672 | tf_op jit(solution)/shard_map/jit(_take)/gather | solution.py:403
  97.9 4.9 %all-to-all-start.1 = ((bf16[4,4,128,1024]{3,2,1,0:T(8,128)(2,1)}), bf16[4,4,128,1024]{3,2,1,0:T(8,128)(2,1)}, u32[]{:S(2)}, u32[]{:S(2)}) async-start(bf16[4,4,128,1024]{3,2,1,0:T(8,128)(2,1)} %bitcast.41), calls=%async_computation.1 | async-start | bytes 8388608 | tf_op jit(solution)/shard_map/all_to_all | solution.py:406
  102.9 48.1 %all-to-all-done.1 = bf16[4,4,128,1024]{3,2,1,0:T(8,128)(2,1)} async-done(((bf16[4,4,128,1024]{3,2,1,0:T(8,128)(2,1)}), bf16[4,4,128,1024]{3,2,1,0:T(8,128)(2,1)}, u32[]{:S(2)}, u32[]{:S(2)}) %all-to-all-start.1) | async-done | bytes 4194336 | tf_op jit(solution)/shard_map/all_to_all | solution.py:406
  151.0 2.9 gather_fusion.1
  153.9 1.3 slice.37
  155.4 37.5 %psum.7 = f32[32,256]{1,0:T(8,128)S(1)} all-reduce(f32[32,256]{1,0:T(8,128)S(1)} %fusion.12), channel_id=1, replica_groups=mesh['dp'=4,'tensor'=8] {'tensor'}, use_global_device_ids=true, to_apply=%region_2.3 | all-reduce | flops 8192 | bytes 65536 | tf_op jit(solution)/shard_map/psum | solution.py:422
  192.9 135.0 %shard_map.73 = (bf16[3,256,512]{2,1,0:T(8,128)(2,1)}, bf16[3,256,512]{2,1,0:T(8,128)(2,1)}) custom-call(bf16[3,256,1024]{2,1,0:T(8,128)(2,1)} %bitcast.44, bf16[8192,512]{1,0:T(8,128)(2,1)} %wk_ref.1, bf16[8192,512]{1,0:T(8,128)(2,1)} %wv_ref.1), custom_call_target="tpu_custom_call" | custom-call | flops 12884901888 | bytes 16777216 | tf_op jit(solution)/shard_map/pallas_call | solution.py:174
  328.5 31.4 %all_gather.15 = bf16[32,8192]{1,0:T(8,128)(2,1)S(1)} all-gather(bf16[32,1024]{1,0:T(8,128)(2,1)S(1)} %convolution_convert_fusion.2), channel_id=1, replica_groups=mesh['dp'=4,'tensor'=8] {'tensor'}, dimensions={1}, use_global_device_ids=true | all-gather | bytes 589824 | tf_op jit(solution)/shard_map/all_gather | solution.py:429
  359.9 4.6 %fusion.5 = bf16[512]{0:T(512)(128)(2,1)S(1)} fusion(bf16[8192,512]{1,0:T(8,128)(2,1)} %wv_ref.1, bf16[32,8192]{1,0:T(8,128)(2,1)S(1)} %all_gather.15, s32[]{:T(128)S(6)} %select_n.68, s32[512]{0:T(512)S(1)} %add_select_fusion), kind=kOutput, calls=%fused_computation.12 | convolution fusion | flops 33560064 | bytes 8457220 | tf_op jit(solution)/shard_map/dot_general | solution.py:437
  364.8 6.4 %fusion.36 = bf16[208,512]{1,0:T(8,128)(2,1)S(1)} fusion(bf16[208,8192]{1,0:T(8,128)(2,1)} %all-gather.3.cloned.1.call-done, bf16[8192,512]{1,0:T(8,128)(2,1)} %param.10), kind=kOutput, calls=%fused_computation.72 | convolution fusion | flops 1744830464 | bytes 12009472 | tf_op jit(solution)/shard_map/dot_general | solution.py:431
  371.3 0.4 convolution_multiply_fusion
  371.7 0.3 fusion.34
  372.0 1.4 fusion.4
  373.7 35.3 %shard_map.74 = bf16[208,1024]{1,0:T(8,128)(2,1)S(1)} custom-call(bf16[208,512]{1,0:T(8,128)(2,1)S(1)} %pad_maximum_fusion.ctx_ref, bf16[512,8192]{1,0:T(8,128)(2,1)} %w_ref.1), custom_call_target="tpu_custom_call" | custom-call | flops 1744830464 | bytes 8388608 | tf_op jit(solution)/shard_map/pallas_call | solution.py:338
  409.1 0.9 concatenate.7
  (37 shorter events, 2.4 us)
Async XLA Ops:
  6.5 358.0 %all-gather.3.cloned.1.call-start = ((), (), s32[]{:S(2)}) async-start(), calls=%async_computation.2 | async-start | bytes 3833856 | tf_op jit(solution)/shard_map/all_gather | solution.py:390
  46.2 37.0 %copy-start.1 = (s32[4,2]{0,1:T(2,128)S(1)}, s32[4,2]{0,1:T(2,128)}, u32[]{:S(2)}) copy-start(s32[4,2]{0,1:T(2,128)} %param.8) | copy-start | bytes 100
  97.9 53.1 %all-to-all-start.1 = ((bf16[4,4,128,1024]{3,2,1,0:T(8,128)(2,1)}), bf16[4,4,128,1024]{3,2,1,0:T(8,128)(2,1)}, u32[]{:S(2)}, u32[]{:S(2)}) async-start(bf16[4,4,128,1024]{3,2,1,0:T(8,128)(2,1)} %bitcast.41), calls=%async_computation.1 | async-start | bytes 8388608 | tf_op jit(solution)/shard_map/all_to_all | solution.py:406
  328.5 36.1 %copy-start = (bf16[3,256,512]{2,1,0:T(8,128)(2,1)S(1)}, bf16[3,256,512]{2,1,0:T(8,128)(2,1)}, u32[]{:S(2)}) copy-start(bf16[3,256,512]{2,1,0:T(8,128)(2,1)} %get-tuple-element.18) | copy-start | bytes 2359300
  364.8 7.2 %copy-start.2 = (bf16[3,256,512]{2,1,0:T(8,128)(2,1)S(1)}, bf16[3,256,512]{2,1,0:T(8,128)(2,1)}, u32[]{:S(2)}) copy-start(bf16[3,256,512]{2,1,0:T(8,128)(2,1)} %get-tuple-element.17) | copy-start | bytes 2359300
Sparse Core Ops, SparseCore 0:
  83.3 64.6 all-gather.2

commit v3 on v2

--- a/solution.py
+++ b/solution.py
@@ -379,15 +379,15 @@
     own_head = (
         jnp.arange(head_cols)[None, :] // HD == jnp.arange(heads_local)[:, None]
     )
-    last_hidden = lax.all_gather(hidden[tok_rows - 16 :], "tensor", axis=1, tiled=True)
-    last_query = jnp.dot(last_hidden, w_query, preferred_element_type=jnp.float32)
-    last_query = jnp.where(own_head, last_query[15:].astype(jnp.bfloat16), 0)
+    all_hidden = lax.all_gather(hidden[skipped:], "tensor", axis=1, tiled=True)
+    query_rows = jnp.dot(
+        all_hidden, w_query, preferred_element_type=jnp.float32
+    ).astype(jnp.bfloat16)
+    last_query = jnp.where(own_head, query_rows[-1:], 0)
     lifted = lax.dot_general(
         last_query, w_key, (((1,), (1,)), ((), ())), preferred_element_type=jnp.float32
     ).astype(jnp.bfloat16)
-    lifted = lax.all_gather(lifted, "tensor", axis=0, tiled=True)
-    late_hidden, lifted = lax.optimization_barrier((hidden[skipped:], lifted))
-    all_hidden = lax.all_gather(late_hidden, "tensor", axis=1, tiled=True)
+    lifted = lax.all_to_all(lifted, "tensor", split_axis=1, concat_axis=0, tiled=True)
     block_ids = neighbour_ids.reshape(per_reader)
     owners = block_ids // db_count
     earlier = jnp.arange(per_reader)[:, None] > jnp.arange(per_reader)[None, :]
@@ -413,27 +413,23 @@
     neighbour_rows = neighbour_rows.reshape(per_reader * ret_len, col_count)
     full_rows = (group_count - 1) * (per_reader // group_count) * ret_len
     last_rows = neighbour_rows[full_rows:]
-    place = lax.axis_index("tensor")
-    lifted = lax.dynamic_slice_in_dim(lifted, place * col_count, col_count, 1)
     last_part = lax.dot_general(
         lifted, last_rows, (((1,), (1,)), ((), ())), preferred_element_type=jnp.float32
     )
     first_rows, last_part = lax.optimization_barrier((neighbour_rows[:full_rows], last_part))
-    last_scores = lax.psum(last_part, "tensor")
+    last_part = jnp.broadcast_to(last_part, (lax.axis_size("tensor"),) + last_part.shape)
+    last_scores = jnp.sum(
+        lax.all_to_all(last_part, "tensor", split_axis=0, concat_axis=0, tiled=True), 0
+    )
     key_rows, value_rows = neighbour_keys(first_rows, w_key, w_value, group_count - 1)
     key_rows, last_scores = lax.optimization_barrier((key_rows, last_scores))
     last_soft = softmax(last_scores / jnp.sqrt(jnp.float32(HD)))
     last_mix = jnp.dot(
         last_soft, last_rows, preferred_element_type=jnp.float32
     ).astype(jnp.bfloat16)
-    last_mix = lax.all_gather(last_mix, "tensor", axis=1, tiled=True)
-    key_rows, all_hidden = lax.optimization_barrier((key_rows, all_hidden))
-    query_rows = jnp.dot(
-        all_hidden, w_query, preferred_element_type=jnp.float32
-    ).astype(jnp.bfloat16)
+    last_mix = lax.all_to_all(last_mix, "tensor", split_axis=0, concat_axis=1, tiled=True)
     lead = group_len - 1 - skipped
     blended = attend(query_rows[lead:-1], key_rows, value_rows, heads_local, group_len)
-    last_mix = lax.dynamic_slice_in_dim(last_mix, place * heads_local, heads_local, 0)
     last_context = jnp.dot(last_mix, w_value, preferred_element_type=jnp.float32)
     last_context = jnp.sum(jnp.where(own_head, last_context, 0), 0, keepdims=True)
     context = jnp.concatenate(

time: 417 us -> 317 us (0.76)
  blocking collectives: 139 us -> 7.76 us
  Pallas kernels: 170 us -> 186 us
  starting transfers between devices: 4.86 us -> 15.7 us
  waiting for transfers between devices: 48.1 us -> 52.3 us
    all_gather x3 -> x0, blocking collectives: 95.1 us -> none  [the longest x1 32.5 us: shards(): lax.all_gather(hidden[tok_rows - 16:], 'tensor', axis=1, tiled=True)]
    all_to_all x1, waiting for transfers between devices: 48.1 us -> 0.01 us  [shards(): lax.all_to_all(outgoing, 'dp', split_axis=0, concat_axis=0, tiled=True)]
    all_gather x1, waiting for transfers between devices: 0.02 us -> 45.6 us  [shards(): all_hidden = lax.all_gather(hidden[skipped:], 'tensor', axis=1, tiled=True)]
    psum x1 -> x0, blocking collectives: 37.5 us -> none  [shards(): last_scores = lax.psum(last_part, 'tensor')]
    all_to_all x0 -> x3, starting transfers between devices: none -> 10.9 us  [the longest x1 4.06 us: shards(): lax.all_to_all(last_mix, 'tensor', split_axis=0, concat_axis=1, tiled=True)]
    pallas_call x1, Pallas kernels: 135 us -> 145 us  [neighbour_keys(): pl.pallas_call(functools.partial(gather_project, nz, ny), out_shape=(out,...]
    all_to_all x0 -> x3, waiting for transfers between devices: none -> 6.65 us  [the longest x1 4.16 us: shards(): lax.all_to_all(last_mix, 'tensor', split_axis=0, concat_axis=1, tiled=True)]
    pallas_call x1, Pallas kernels: 35.3 us -> 40.6 us  [project_out(): pl.pallas_call(functools.partial(project_scatter, nz, ny), out_shape=jax....]
  transfers between devices with their start and end apart: 2 -> 5, of which waited for: 1 -> 3; matrix products, arithmetic and copies ran while one was open for 4% -> 9% of each run, Pallas kernels for 32% -> 46%
where the time goes in v3:
time: 317 us; the launch traced here: 316 us
  Pallas kernels  186 us (59%)
  waiting for transfers between devices  52.3 us (16%)
  matrix products  20.6 us (6%)
  local copies, waits for them, and re-layouts  18.5 us (6%)
  starting transfers between devices  15.7 us (5%)
  between operations  13.6 us (4%)
  blocking collectives  7.76 us (2%)
    pallas_call x1, Pallas kernels, neighbour_keys(): pl.pallas_call(functools.partial(gather_project, nz, ny), out_shape=(out,...  145 us
    all_gather x1, waiting for transfers between devices, shards(): all_hidden = lax.all_gather(hidden[skipped:], 'tensor', axis=1, tiled=True)  45.6 us
    pallas_call x1, Pallas kernels, project_out(): pl.pallas_call(functools.partial(project_scatter, nz, ny), out_shape=jax....  40.6 us
    all_to_all x1, blocking collectives, shards(): lax.all_to_all(request_table, 'dp', split_axis=0, concat_axis=0, tiled=True)  7.76 us
    gather x1, local copies, waits for them, and re-layouts, shards(): jnp.take(database, requested.reshape(-1), axis=0, mode='clip')  6.53 us
  transfers between devices with their start and end apart: 5, of which 3 were waited for; matrix products, arithmetic and copies ran while one was open for 9% of the time, Pallas kernels for 46%

profile of v3, /device:TPU:0, one launch (start us, length us, event | category | flops | bytes accessed | tf_op | source)
XLA Modules:
  0.0 315.9 jit_solution(607934042879448302)
XLA Ops:
  6.5 1.8 slice.23
  8.4 0.8 copy.28
  9.6 7.8 %all_to_all.57 = s32[4,1,4]{2,1,0:T(1,128)S(1)} all-to-all(s32[4,1,4]{2,1,0:T(1,128)S(1)} %bitcast.53), channel_id=1, replica_groups=mesh['dp'=4,'tensor'=8] {'dp'}, dimensions={0} | all-to-all | bytes 128 | tf_op jit(solution)/shard_map/all_to_all | solution.py:402
  17.9 0.7 reduce.5
  18.7 6.5 %gather_fusion = bf16[16,128,1024]{2,1,0:T(8,128)(2,1)} fusion(bf16[32,128,1024]{2,1,0:T(8,128)(2,1)} %param.9, s32[1024]{0:T(1024)S(1)} %pad_clamp_fusion.1), kind=kCustom, calls=%fused_computation | custom fusion | bytes 8388672 | tf_op jit(solution)/shard_map/jit(_take)/gather | solution.py:403
  25.3 4.9 %all-to-all-start.1 = ((bf16[4,4,128,1024]{3,2,1,0:T(8,128)(2,1)}), bf16[4,4,128,1024]{3,2,1,0:T(8,128)(2,1)}, u32[]{:S(2)}, u32[]{:S(2)}) async-start(bf16[4,4,128,1024]{3,2,1,0:T(8,128)(2,1)} %bitcast.44), calls=%async_computation.1 | async-start | bytes 8388608 | tf_op jit(solution)/shard_map/all_to_all | solution.py:406
  30.2 45.6 %all-gather.2.cloned.1.call-done = bf16[208,8192]{1,0:T(8,128)(2,1)} async-done(((bf16[208,1024]{1,0:T(8,128)(2,1)}), bf16[208,8192]{1,0:T(8,128)(2,1)}) %all-gather.2.cloned.1.call-update) | async-done | bytes 3407888 | tf_op jit(solution)/shard_map/all_gather | solution.py:382
  75.8 6.3 %convolution_convert_fusion.1 = bf16[208,512]{1,0:T(8,128)(2,1)S(1)} fusion(bf16[208,8192]{1,0:T(8,128)(2,1)} %all-gather.2.cloned.1.call-done, bf16[8192,512]{1,0:T(8,128)(2,1)} %param.10), kind=kOutput, calls=%fused_computation.7 | convolution fusion | flops 1744936960 | bytes 12009472 | tf_op jit(solution)/shard_map/dot_general | solution.py:383
  82.2 6.3 %convolution_convert_fusion = bf16[4,8192]{1,0:T(4,128)(2,1)} fusion(bf16[8192,512]{1,0:T(8,128)(2,1)} %wk_ref.1, s32[512]{0:T(512)S(1)} %add_select_fusion, bf16[512]{0:T(512)(128)(2,1)S(1)} %slice_reduce_fusion), kind=kOutput, calls=%fused_computation.3 | convolution fusion | flops 33591296 | bytes 8457216 | tf_op jit(solution)/shard_map/dot_general | solution.py:387
  88.5 3.4 %all-to-all-start.2 = ((bf16[4,8,1024]{2,0,1:T(4,128)(2,1)}), bf16[4,8,1024]{2,0,1:T(4,128)(2,1)S(1)}, u32[]{:S(2)}, u32[]{:S(2)}) async-start(bf16[4,8,1024]{2,0,1:T(4,128)(2,1)} %bitcast.7), calls=%async_computation.2 | async-start | bytes 131072 | tf_op jit(solution)/shard_map/all_to_all | solution.py:390
  91.9 2.9 gather_fusion.1
  94.8 1.3 slice.33
  96.2 2.5 all-to-all-done.2
  99.0 0.7 broadcast_in_dim.52
  99.7 3.5 %all-to-all-start.3 = ((f32[8,32,256]{2,1,0:T(8,128)}), f32[8,32,256]{2,1,0:T(8,128)S(1)}, u32[]{:S(2)}, u32[]{:S(2)}) async-start(f32[8,32,256]{2,1,0:T(8,128)} %broadcast_in_dim.52), calls=%async_computation.3 | async-start | bytes 524288 | tf_op jit(solution)/shard_map/all_to_all | solution.py:422
  103.2 145.0 %shard_map.73 = (bf16[3,256,512]{2,1,0:T(8,128)(2,1)}, bf16[3,256,512]{2,1,0:T(8,128)(2,1)}) custom-call(bf16[3,256,1024]{2,1,0:T(8,128)(2,1)} %bitcast.47, bf16[8192,512]{1,0:T(8,128)(2,1)} %wk_ref.1, bf16[8192,512]{1,0:T(8,128)(2,1)} %wv_ref.1), custom_call_target="tpu_custom_call" | custom-call | flops 12884901888 | bytes 16777216 | tf_op jit(solution)/shard_map/pallas_call | solution.py:174
  248.2 1.8 reshape.308
  251.2 0.7 all_to_all.48
  251.9 4.1 %all-to-all-start.4 = ((bf16[8,4,1024]{2,1,0:T(4,128)(2,1)}), bf16[8,4,1024]{2,1,0:T(4,128)(2,1)S(1)}, u32[]{:S(2)}, u32[]{:S(2)}) async-start(bf16[8,4,1024]{2,1,0:T(4,128)(2,1)} %all_to_all.48), calls=%async_computation.4 | async-start | bytes 131072 | tf_op jit(solution)/shard_map/all_to_all | solution.py:430
  255.9 2.5 fusion.3
  258.7 4.2 %all-to-all-done.4 = bf16[8,4,1024]{2,1,0:T(4,128)(2,1)S(1)} async-done(((bf16[8,4,1024]{2,1,0:T(4,128)(2,1)}), bf16[8,4,1024]{2,1,0:T(4,128)(2,1)S(1)}, u32[]{:S(2)}, u32[]{:S(2)}) %all-to-all-start.4) | async-done | bytes 65568 | tf_op jit(solution)/shard_map/all_to_all | solution.py:430
  262.9 4.6 %fusion.4 = bf16[512]{0:T(512)(128)(2,1)S(1)} fusion(bf16[4,8192]{1,0:T(4,128)(2,1)S(1)} %bitcast.51, bf16[8192,512]{1,0:T(8,128)(2,1)} %wv_ref.1, s32[512]{0:T(512)S(1)} %add_select_fusion), kind=kOutput, calls=%fused_computation.12 | convolution fusion | flops 33560064 | bytes 8457216 | tf_op jit(solution)/shard_map/dot_general | solution.py:433
  267.6 40.6 %shard_map.74 = bf16[208,1024]{1,0:T(8,128)(2,1)S(1)} custom-call(bf16[208,512]{1,0:T(8,128)(2,1)S(1)} %pad_maximum_fusion.ctx_ref, bf16[512,8192]{1,0:T(8,128)(2,1)} %w_ref.1), custom_call_target="tpu_custom_call" | custom-call | flops 1744830464 | bytes 8388608 | tf_op jit(solution)/shard_map/pallas_call | solution.py:338
  308.2 0.9 concatenate.7
  (34 shorter events, 3.2 us)
Async XLA Ops:
  6.5 69.3 %all-gather.2.cloned.1.call-start = ((), (), s32[]{:S(2)}) async-start(), calls=%async_computation.5 | async-start | bytes 3833856 | tf_op jit(solution)/shard_map/all_gather | solution.py:382
  25.3 63.2 %all-to-all-start.1 = ((bf16[4,4,128,1024]{3,2,1,0:T(8,128)(2,1)}), bf16[4,4,128,1024]{3,2,1,0:T(8,128)(2,1)}, u32[]{:S(2)}, u32[]{:S(2)}) async-start(bf16[4,4,128,1024]{3,2,1,0:T(8,128)(2,1)} %bitcast.44), calls=%async_computation.1 | async-start | bytes 8388608 | tf_op jit(solution)/shard_map/all_to_all | solution.py:406
  88.5 10.2 %all-to-all-start.2 = ((bf16[4,8,1024]{2,0,1:T(4,128)(2,1)}), bf16[4,8,1024]{2,0,1:T(4,128)(2,1)S(1)}, u32[]{:S(2)}, u32[]{:S(2)}) async-start(bf16[4,8,1024]{2,0,1:T(4,128)(2,1)} %bitcast.7), calls=%async_computation.2 | async-start | bytes 131072 | tf_op jit(solution)/shard_map/all_to_all | solution.py:390
  99.7 148.5 %all-to-all-start.3 = ((f32[8,32,256]{2,1,0:T(8,128)}), f32[8,32,256]{2,1,0:T(8,128)S(1)}, u32[]{:S(2)}, u32[]{:S(2)}) async-start(f32[8,32,256]{2,1,0:T(8,128)} %broadcast_in_dim.52), calls=%async_computation.3 | async-start | bytes 524288 | tf_op jit(solution)/shard_map/all_to_all | solution.py:422
  251.9 11.0 %all-to-all-start.4 = ((bf16[8,4,1024]{2,1,0:T(4,128)(2,1)}), bf16[8,4,1024]{2,1,0:T(4,128)(2,1)S(1)}, u32[]{:S(2)}, u32[]{:S(2)}) async-start(bf16[8,4,1024]{2,1,0:T(4,128)(2,1)} %all_to_all.48), calls=%async_computation.4 | async-start | bytes 131072 | tf_op jit(solution)/shard_map/all_to_all | solution.py:430
Sparse Core Ops, SparseCore 0:
  9.5 66.2 all-gather.1
